TPU v7x, 32 devices: a whole 2x2x4 slice. The times are simulated.
32 devices in a mesh: groups: 2 (over x), clus: 16 (over z, y, core).
Axes of the slice: x: 2, y: 2, z: 4, core: 2. Of those that a mesh axis runs over, the one named last changes fastest.
Arguments:
- mesh_current: float32 [2, 131072], P(None, ('groups', 'clus')), parts along dimension 1, may hold values from -6 to 6
- branch_entry: int32 [2, 262144], P(None, ('groups', 'clus')), parts along dimension 1, may hold values from 0 to 6143, as said below
- branch_sign: int32 [2, 262144], P(None, ('groups', 'clus')), parts along dimension 1, may hold values from 0 to 1
- need_slots: int32 [512, 128], P(('groups', 'clus')), parts along dimension 0, may hold values from -1 to 4095, as said below
- resistance: float32 [262144], P(('groups', 'clus')), parts along dimension 0, may hold values from 0.3 to 3
- near_blocks: bfloat16 [2048, 4, 128, 128], P(('groups', 'clus')), parts along dimension 0, may hold values from -0.25 to 0.25
- near_source: int32 [2048, 4], P(('groups', 'clus')), parts along dimension 0, may hold values from 0 to 63
- basis_in: bfloat16 [2048, 32, 128], P(('groups', 'clus')), parts along dimension 0, may hold values from -0.5 to 0.5
- coupling: bfloat16 [2048, 16, 32, 32], P(('groups', 'clus')), parts along dimension 0, may hold values from -0.25 to 0.25
- basis_out: bfloat16 [2048, 32, 128], P(('groups', 'clus')), parts along dimension 0, may hold values from -1 to 1
- admissible: int32 [2048, 16], P(('groups', 'clus')), parts along dimension 0, may hold values from 0 to 1023, as said below
- port_mesh: int32 [128], P('groups'), parts along dimension 0, may hold values from 0 to 65535, as said below
- port_coupling: float32 [2, 64, 64], replicated, may hold values from -0.75 to 0.75
Outputs:
- mesh_voltage: float32 [2, 131072], P(None, ('groups', 'clus')), parts along dimension 1
There are 2 independent parts, one for each index of `groups`. A program takes and returns all parts, laid end to end along the dimension named above; an argument that names none is the same for every part. Nothing has to cross between parts.
Inputs may be any that keep to these rules, and one draw needn't show every extreme that they name: `need_slots`: row d * 16 + p holds distinct meshes of device p, counted from 0 within it, in its first slots and -1 in the rest. Row d * 16 + d is all -1; row d * 16 + (d + 1) % 16 has no -1. `branch_entry`: A value below 4096 is a mesh of the branch's own device d. Any other value is 4096 + p * 128 + s with p != d and slot s of row d * 16 + p of need_slots not -1. `admissible`: entry k of row t is (t + k * 64 + o) % 1024 with 1 <= o < 64; the entries of a row are distinct and never t. `port_mesh`: distinct meshes.
All inputs are finite; a program needn't handle non-finite values.
Results may differ from a plain program's by a relative error of at most 0.0021.
Values may be sent and summed in bfloat16 or wider, within the bound.
A program may use at most 320 MiB of HBM per device.

v0:
```python
import jax
import jax.numpy as jnp
from jax import lax
from jax.sharding import PartitionSpec as P


def segment_sums(values, segment_ids, total):

    def one_part(part_values):
        return jax.ops.segment_sum(part_values, segment_ids, num_segments=total)

    return jax.vmap(one_part)(values)


def per_device(
    mesh_current,
    branch_entry,
    branch_sign,
    need_slots,
    resistance,
    near_blocks,
    near_source,
    basis_in,
    coupling,
    basis_out,
    admissible,
    port_mesh,
    port_coupling,
):
    peer_count = lax.axis_size("clus")
    mesh_dev = mesh_current.shape[1]
    slot_width = need_slots.shape[1]
    tile_dev = near_blocks.shape[0]
    tile_width = near_blocks.shape[2]
    offset = lax.axis_index("clus") * mesh_dev
    position = port_mesh - offset
    owned = (position >= 0) & (position < mesh_dev)
    owner_base = (jnp.arange(peer_count, dtype=jnp.int32) * mesh_dev)[:, None]
    slot_mesh = (owner_base + jnp.maximum(need_slots, 0)).reshape(-1)
    all_currents = lax.all_gather(mesh_current, "clus", axis=1, tiled=True)
    remote = all_currents[:, slot_mesh]
    port_value = all_currents[:, port_mesh]
    lookup_table = jnp.concatenate([mesh_current, remote], axis=1)
    orient = (2 * branch_sign - 1).astype(jnp.float32)
    branch_current = jnp.sum(orient[None] * lookup_table[:, branch_entry], axis=1)
    branch_input = branch_current.astype(jnp.bfloat16).reshape(2, tile_dev, tile_width)
    far_coeff = jnp.einsum(
        "tri,cti->ctr", basis_in, branch_input, preferred_element_type=jnp.float32
    ).astype(jnp.bfloat16)
    all_coeff = lax.all_gather(far_coeff, "clus", axis=1, tiled=True)
    near_input = branch_input[:, near_source]
    near_field = jnp.einsum(
        "tkij,ctkj->cti", near_blocks, near_input, preferred_element_type=jnp.float32
    )
    picked = all_coeff[:, admissible]
    far_mixed = jnp.einsum(
        "tkrq,ctkq->ctr", coupling, picked, preferred_element_type=jnp.float32
    ).astype(jnp.bfloat16)
    far_field = jnp.einsum("tri,ctr->cti", basis_out, far_mixed, preferred_element_type=jnp.float32)
    reactive = (near_field + far_field).reshape(2, -1)
    branch_voltage = resistance[None, :] * branch_current + jnp.stack([-reactive[1], reactive[0]])
    contributions = (orient[None] * branch_voltage[:, None, :]).reshape(2, -1)
    totals = segment_sums(
        contributions, branch_entry.reshape(-1), mesh_dev + peer_count * slot_width
    )
    local_voltage = totals[:, :mesh_dev]
    slot_voltage = totals[:, mesh_dev:]
    spread = jnp.zeros((2, peer_count * mesh_dev), jnp.float32).at[:, slot_mesh].add(slot_voltage)
    arrived = lax.psum_scatter(spread, "clus", scatter_dimension=1, tiled=True)
    mesh_voltage = local_voltage + arrived
    high = lax.Precision.HIGHEST
    real_part = jnp.dot(port_coupling[0], port_value[0], precision=high) - jnp.dot(
        port_coupling[1], port_value[1], precision=high
    )
    imag_part = jnp.dot(port_coupling[0], port_value[1], precision=high) + jnp.dot(
        port_coupling[1], port_value[0], precision=high
    )
    target_rows = jnp.where(owned, position, mesh_dev)
    mesh_voltage = mesh_voltage.at[:, target_rows].add(
        jnp.stack([real_part, imag_part]), mode="drop"
    )
    return mesh_voltage


def solution(mesh):
    in_specs = (
        P(None, ("groups", "clus")),
        P(None, ("groups", "clus")),
        P(None, ("groups", "clus")),
        P(("groups", "clus"), None),
        P(("groups", "clus")),
        P(("groups", "clus"), None, None, None),
        P(("groups", "clus"), None),
        P(("groups", "clus"), None, None),
        P(("groups", "clus"), None, None, None),
        P(("groups", "clus"), None, None),
        P(("groups", "clus"), None),
        P("groups"),
        P(),
    )
    out_specs = P(None, ("groups", "clus"))
    return jax.shard_map(
        per_device, mesh=mesh, in_specs=in_specs, out_specs=out_specs, check_vma=False
    )
```

profile of v0, /device:TPU:0, one launch (start us, length us, event | category | flops | bytes accessed | tf_op | source)
XLA Modules:
  0.0 998.2 jit_solution(3522552970147552140)
XLA Ops:
  6.5 0.7 compare_select_fusion.3
  7.3 0.8 maximum_add_fusion
  8.1 0.7 compare_select_fusion.2
  9.2 0.9 fusion.15
  10.1 0.8 copy.62
  10.9 0.9 fusion.29
  11.8 1.4 copy.50
  13.2 13.3 %copy.55 = bf16[64,16,32,32]{3,2,1,0:T(8,128)(2,1)} copy(bf16[64,16,32,32]{0,3,2,1:T(8,128)(2,1)} %param.21) | data formatting | bytes 4194304 | tf_op args[8]
  26.6 331.8 %all_gather.6 = f32[2,65536]{0,1:T(8,128)} all-gather(f32[2,4096]{0,1:T(8,128)S(1)} %copy.50), channel_id=1, replica_groups=mesh['groups'=2,'clus'=16] {'clus'}, dimensions={1}, use_global_device_ids=true | all-gather | bytes 557056 | tf_op jit(solution)/shard_map/all_gather | solution.py:40
  358.4 18.1 %gather_fusion = f32[2048,2]{1,0:T(8,128)} fusion(f32[2,65536]{0,1:T(8,128)} %all_gather.6, s32[2048]{0:T(1024)S(1)} %broadcast_clamp_fusion.1), kind=kCustom, calls=%fused_computation | custom fusion | bytes 40960 | tf_op jit(solution)/shard_map/gather | solution.py:41
  376.5 3.0 pad_maximum_fusion
  379.5 56.3 %gather_fusion.1 = f32[16384,2]{1,0:T(8,128)} fusion(f32[2,6144]{0,1:T(8,128)} %pad_maximum_fusion, s32[16384]{0:T(1024)S(1)} %broadcast_clamp_fusion), kind=kCustom, calls=%fused_computation.1 | custom fusion | bytes 327680 | tf_op jit(solution)/shard_map/gather | solution.py:45
  435.8 5.5 multiply_reduce_fusion
  441.5 1.2 copy-done.3
  442.7 0.7 fusion.10
  443.4 63.3 %all_gather.7 = bf16[2,1024,32]{2,0,1:T(2,128)(2,1)S(1)} all-gather(bf16[2,64,32]{2,0,1:T(2,128)(2,1)S(1)} %fusion.10), channel_id=1, replica_groups=mesh['groups'=2,'clus'=16] {'clus'}, dimensions={1}, use_global_device_ids=true | all-gather | bytes 139264 | tf_op jit(solution)/shard_map/all_gather | solution.py:50
  506.7 8.6 gather_fusion.2
  515.3 6.4 copy.52
  521.7 3.7 gather_fusion.3
  525.4 5.8 fusion.9
  531.1 5.7 fusion.6
  537.0 2.7 copy.56
  539.7 4.1 bitcast_add_fusion
  543.8 4.6 bitcast_multiply_fusion
  548.4 81.5 %scatter_custom_fusion = f32[2,6144]{0,1:T(8,128)} fusion(s32[16384]{0:T(1024)S(1)} %bitcast.119, f32[2,16384]{0,1:T(8,128)} %bitcast_multiply_fusion, f32[]{:T(128)} %constant.10.clone.1), kind=kCustom, calls=%fused_computation.10 | custom fusion | flops 32768 | bytes 180228 | tf_op jit(solution)/shard_map/vmap()/scatter-add | solution.py:10
  630.0 25.9 %scatter_custom_fusion.1 = f32[2,65536]{0,1:T(8,128)} fusion(s32[2048]{0:T(1024)S(1)} %bitcast.121, f32[]{:T(128)} %constant.10.clone.1, f32[2,6144]{0,1:T(8,128)} %scatter_custom_fusion), kind=kCustom, calls=%fused_computation.8 | custom fusion | flops 4096 | bytes 1573376 | tf_op jit(solution)/shard_map/scatter-add | solution.py:68
  655.8 0.6 copy-done.6
  656.5 16.2 %gather_fusion.4 = f32[64,2]{1,0:T(8,128)S(1)} fusion(f32[2,65536]{0,1:T(8,128)} %all_gather.6, s32[1024]{0:T(1024)S(1)} %pad_clamp_fusion), kind=kCustom, calls=%fused_computation.4 | custom fusion | bytes 1280 | tf_op jit(solution)/shard_map/gather | solution.py:42
  673.7 312.3 %reduce-scatter.2.cloned.1.call-done = f32[2,4096]{0,1:T(8,128)} async-done(((f32[2,65536]{0,1:T(8,128)}), f32[2,4096]{0,1:T(8,128)}) %reduce-scatter.2.cloned.1.call-update) | async-done | bytes 32784 | tf_op jit(solution)/shard_map/reduce_scatter | solution.py:69
  986.0 2.4 slice_add_fusion
  988.4 1.7 scatter_fusion
  990.1 1.2 copy.58
  (38 shorter events, 1.8 us)
Async XLA Ops:
  6.5 518.8 %copy-start = (bf16[64,32,128]{2,1,0:T(8,128)(2,1)S(1)}, bf16[64,32,128]{2,1,0:T(8,128)(2,1)}, u32[]{:S(2)}) copy-start(bf16[64,32,128]{2,1,0:T(8,128)(2,1)} %param.22) | copy-start | bytes 1572868
  6.5 979.4 %reduce-scatter.2.cloned.1.call-start = ((), (), s32[]{:S(2)}) async-start(), calls=%async_computation.1 | async-start | bytes 35651584 | tf_op jit(solution)/shard_map/reduce_scatter | solution.py:69
  441.3 2.1 copy-start.2
  441.3 1.4 copy-start.3
  536.8 2.9 copy-start.5
  655.8 0.7 copy-start.6
  655.8 17.0 %copy-start.4 = (f32[2,64,64]{2,1,0:T(8,128)S(1)}, f32[2,64,64]{2,1,0:T(8,128)}, u32[]{:S(2)}) copy-start(f32[2,64,64]{2,1,0:T(8,128)} %param.25) | copy-start | bytes 98308
  673.6 317.8 %copy-start.1 = (bf16[64,32,128]{2,1,0:T(8,128)(2,1)S(1)}, bf16[64,32,128]{2,1,0:T(8,128)(2,1)}, u32[]{:S(2)}) copy-start(bf16[64,32,128]{2,1,0:T(8,128)(2,1)} %param.22) | copy-start | bytes 1572868
Sparse Core Ops, SparseCore 0:
  656.0 329.9 reduce-scatter.1
where the time goes:
time: 999 us; the launch traced here: 998 us
  blocking collectives  395 us (40%)
  waiting for transfers between devices  312 us (31%)
  other arithmetic  133 us (13%)
  local copies, waits for them, and re-layouts  131 us (13%)
  between operations  13.6 us (1%)
  matrix products  12.8 us (1%)
    all_gather x1, blocking collectives, per_device(): all_currents = lax.all_gather(mesh_current, 'clus', axis=1, tiled=True)  332 us
    reduce_scatter x1, waiting for transfers between devices, per_device(): arrived = lax.psum_scatter(spread, 'clus', scatter_dimension=1, tiled=True)  312 us
    scatter-add x1, other arithmetic, one_part(): return jax.ops.segment_sum(part_values, segment_ids, num_segments=total)  81.5 us
    all_gather x1, blocking collectives, per_device(): all_coeff = lax.all_gather(far_coeff, 'clus', axis=1, tiled=True)  63.3 us
    gather x1, local copies, waits for them, and re-layouts, per_device(): lookup_table[:, branch_entry]  56.3 us
    scatter-add x1, other arithmetic, per_device(): jnp.zeros((2, peer_count * mesh_dev), jnp.float32).at[:, slot_mesh]  25.9 us
  transfers between devices with their start and end apart: 1, of which 1 were waited for; matrix products, arithmetic and copies ran while one was open for 2% of the time, Pallas kernels for 0%

commit v1 on v0

--- a/solution.py
+++ b/solution.py
@@ -37,7 +37,12 @@
     owned = (position >= 0) & (position < mesh_dev)
     owner_base = (jnp.arange(peer_count, dtype=jnp.int32) * mesh_dev)[:, None]
     slot_mesh = (owner_base + jnp.maximum(need_slots, 0)).reshape(-1)
-    all_currents = lax.all_gather(mesh_current, "clus", axis=1, tiled=True)
+    ring = [mesh_current]
+    for hop in range(15):
+        ring.append(lax.ppermute(ring[-1], "clus", [(dev, (dev + 1) % 16) for dev in range(16)]))
+    all_currents = jnp.roll(
+        jnp.concatenate(ring[::-1], axis=1), (lax.axis_index("clus") + 1) * ring[0].shape[1], axis=1
+    )
     remote = all_currents[:, slot_mesh]
     port_value = all_currents[:, port_mesh]
     lookup_table = jnp.concatenate([mesh_current, remote], axis=1)

time: 999 us -> 723 us (0.72)
  blocking collectives: 395 us -> 19.6 us
  waiting for transfers between devices: 312 us -> 396 us
  local copies, waits for them, and re-layouts: 131 us -> 145 us
    all_gather x1 -> x0, blocking collectives: 332 us -> none  [per_device(): all_currents = lax.all_gather(mesh_current, 'clus', axis=1, tiled=True)]
    ppermute x0 -> x15, waiting for transfers between devices: none -> 79.7 us  [per_device(): lax.ppermute(ring[-1], 'clus', [(dev, (dev + 1) % 16) for dev in range(16)])]
    all_gather x1, blocking collectives: 63.3 us -> 19.6 us  [per_device(): all_coeff = lax.all_gather(far_coeff, 'clus', axis=1, tiled=True)]
    unnamed x19 -> x57, local copies, waits for them, and re-layouts: 17.4 us -> 31.9 us
  transfers between devices with their start and end apart: 1 -> 16, of which waited for: 1 -> 15; matrix products, arithmetic and copies ran while one was open for 2% -> 5% of each run, Pallas kernels for 0% -> 0%
where the time goes in v1:
time: 723 us; the launch traced here: 722 us
  waiting for transfers between devices  396 us (55%)
  local copies, waits for them, and re-layouts  145 us (20%)
  other arithmetic  135 us (19%)
  blocking collectives  19.6 us (3%)
  between operations  13.8 us (2%)
  matrix products  12.8 us (2%)
    reduce_scatter x1, waiting for transfers between devices, per_device(): arrived = lax.psum_scatter(spread, 'clus', scatter_dimension=1, tiled=True)  316 us
    scatter-add x1, other arithmetic, one_part(): return jax.ops.segment_sum(part_values, segment_ids, num_segments=total)  81.6 us
    ppermute x15, waiting for transfers between devices, per_device(): lax.ppermute(ring[-1], 'clus', [(dev, (dev + 1) % 16) for dev in range(16)])  79.7 us
    gather x1, local copies, waits for them, and re-layouts, per_device(): lookup_table[:, branch_entry]  56.7 us
    unnamed x57, local copies, waits for them, and re-layouts  31.9 us
    scatter-add x1, other arithmetic, per_device(): jnp.zeros((2, peer_count * mesh_dev), jnp.float32).at[:, slot_mesh]  25.9 us
    all_gather x1, blocking collectives, per_device(): all_coeff = lax.all_gather(far_coeff, 'clus', axis=1, tiled=True)  19.6 us
    gather x1, local copies, waits for them, and re-layouts, per_device(): remote = all_currents[:, slot_mesh]  18.2 us
  transfers between devices with their start and end apart: 16, of which 15 were waited for; matrix products, arithmetic and copies ran while one was open for 5% of the time, Pallas kernels for 0%

profile of v1, /device:TPU:0, one launch (start us, length us, event | category | flops | bytes accessed | tf_op | source)
XLA Modules:
  0.0 722.4 jit_solution(8487447033574389579)
XLA Ops:
  7.0 6.8 collective-permute-done
  13.8 6.0 collective-permute-done.1
  19.8 6.0 collective-permute-done.2
  26.8 5.1 collective-permute-done.3
  31.9 6.0 collective-permute-done.4
  37.9 6.0 collective-permute-done.5
  44.8 5.3 collective-permute-done.6
  50.0 6.0 collective-permute-done.7
  56.9 5.1 collective-permute-done.8
  62.1 6.0 collective-permute-done.9
  69.0 5.2 collective-permute-done.10
  74.2 6.0 collective-permute-done.11
  80.9 5.3 collective-permute-done.12
  87.6 4.7 collective-permute-done.13
  94.3 13.4 %copy.59 = bf16[64,16,32,32]{3,2,1,0:T(8,128)(2,1)} copy(bf16[64,16,32,32]{0,3,2,1:T(8,128)(2,1)} %param.21) | data formatting | bytes 4194304 | tf_op args[8]
  108.3 15.6 %copy.66 = f32[2,65536]{0,1:T(8,128)} copy(f32[2,65536]{1,0:T(2,128)S(1)} %constant_dynamic-slice_fusion) | data formatting | bytes 1048576
  123.9 18.2 %gather_fusion = f32[2048,2]{1,0:T(8,128)} fusion(f32[2,65536]{0,1:T(8,128)} %copy.66, s32[2048]{0:T(1024)S(1)} %broadcast_clamp_fusion.1), kind=kCustom, calls=%fused_computation | custom fusion | bytes 40960 | tf_op jit(solution)/shard_map/gather | solution.py:46
  142.0 3.1 pad_maximum_fusion
  145.1 56.7 %gather_fusion.1 = f32[16384,2]{1,0:T(8,128)} fusion(f32[2,6144]{0,1:T(8,128)} %pad_maximum_fusion, s32[16384]{0:T(1024)S(1)} %broadcast_clamp_fusion), kind=kCustom, calls=%fused_computation.1 | custom fusion | bytes 327680 | tf_op jit(solution)/shard_map/gather | solution.py:50
  201.8 5.5 multiply_reduce_fusion
  209.4 19.6 %all_gather.3 = bf16[2,1024,32]{2,0,1:T(2,128)(2,1)S(1)} all-gather(bf16[2,64,32]{2,0,1:T(2,128)(2,1)S(1)} %fusion.10), channel_id=1, replica_groups=mesh['groups'=2,'clus'=16] {'clus'}, dimensions={1}, use_global_device_ids=true | all-gather | bytes 139264 | tf_op jit(solution)/shard_map/all_gather | solution.py:55
  229.0 8.6 %gather_fusion.2 = bf16[256,2,128]{1,2,0:T(8,128)(2,1)} fusion(bf16[2,64,128]{0,2,1:T(8,128)(2,1)S(1)} %bitcast.110, s32[1024]{0:T(1024)S(1)} %get-tuple-element.14), kind=kCustom, calls=%fused_computation.2 | custom fusion | bytes 263168 | tf_op jit(solution)/shard_map/gather | solution.py:56
  237.6 6.4 copy.56
  244.0 3.7 gather_fusion.3
  247.7 5.8 fusion.9
  253.5 5.7 fusion.6
  262.1 4.1 bitcast_add_fusion
  266.2 4.6 bitcast_multiply_fusion
  270.9 81.6 %scatter_custom_fusion = f32[2,6144]{0,1:T(8,128)} fusion(s32[16384]{0:T(1024)S(1)} %bitcast.119, f32[2,16384]{0,1:T(8,128)} %bitcast_multiply_fusion, f32[]{:T(128)} %constant.15.clone.1), kind=kCustom, calls=%fused_computation.10 | custom fusion | flops 32768 | bytes 180228 | tf_op jit(solution)/shard_map/vmap()/scatter-add | solution.py:10
  352.4 25.9 %scatter_custom_fusion.1 = f32[2,65536]{0,1:T(8,128)} fusion(s32[2048]{0:T(1024)} %bitcast.121, f32[]{:T(128)} %constant.15.clone.1, f32[2,6144]{0,1:T(8,128)} %scatter_custom_fusion), kind=kCustom, calls=%fused_computation.8 | custom fusion | flops 4096 | bytes 1573376 | tf_op jit(solution)/shard_map/scatter-add | solution.py:73
  378.3 14.9 %gather_fusion.4 = f32[64,2]{1,0:T(8,128)S(1)} fusion(f32[2,65536]{0,1:T(8,128)} %copy.66, s32[1024]{0:T(1024)} %get-tuple-element.13), kind=kCustom, calls=%fused_computation.4 | custom fusion | bytes 1280 | tf_op jit(solution)/shard_map/gather | solution.py:47
  394.2 316.0 %reduce-scatter.2.cloned.1.call-done = f32[2,4096]{0,1:T(8,128)} async-done(((f32[2,65536]{0,1:T(8,128)}), f32[2,4096]{0,1:T(8,128)}) %reduce-scatter.2.cloned.1.call-update) | async-done | bytes 32784 | tf_op jit(solution)/shard_map/reduce_scatter | solution.py:74
  (106 shorter events, 19.7 us)
Async XLA Ops:
  6.5 241.1 %copy-start = (bf16[64,32,128]{2,1,0:T(8,128)(2,1)S(1)}, bf16[64,32,128]{2,1,0:T(8,128)(2,1)}, u32[]{:S(2)}) copy-start(bf16[64,32,128]{2,1,0:T(8,128)(2,1)} %param.22) | copy-start | bytes 1572868
  6.5 703.6 %reduce-scatter.2.cloned.1.call-start = ((), (), s32[]{:S(2)}) async-start(), calls=%async_computation.1 | async-start | bytes 35651584 | tf_op jit(solution)/shard_map/reduce_scatter | solution.py:74
  6.5 7.3 %collective-permute-start = (f32[2,4096]{1,0:T(2,128)}, f32[2,4096]{1,0:T(2,128)S(1)}, u32[]{:S(2)}, u32[]{:S(2)}) collective-permute-start(f32[2,4096]{1,0:T(2,128)} %param.13), channel_id=1, source_target_pairs={{0,1},{1,2},{2,3},{3,4},{4,5},{5,6},{6,7},{7,8},{8,9},{9,10},{10,1... | collective-permute-start | bytes 98312 | tf_op jit(solution)/shard_map/ppermute | solution.py:42
  13.8 6.0 collective-permute-start.1
  19.8 6.0 collective-permute-start.2
  25.9 6.0 collective-permute-start.3
  31.9 6.0 collective-permute-start.4
  37.9 6.0 collective-permute-start.5
  44.0 6.0 collective-permute-start.6
  50.0 6.0 collective-permute-start.7
  50.0 12.1 %copy-start.8 = (s32[2048,1]{0,1:T(1,128)}, s32[2048,1]{0,1:T(1,128)S(1)}, u32[]{:S(2)}) copy-start(s32[2048,1]{0,1:T(1,128)S(1)} %compare_select_fusion.1) | copy-start | bytes 24580
  56.1 6.0 collective-permute-start.8
  62.1 6.0 collective-permute-start.9
  68.1 6.0 collective-permute-start.10
  74.2 6.0 collective-permute-start.11
  80.2 6.0 collective-permute-start.12
  86.2 6.0 collective-permute-start.13
  92.3 15.5 %collective-permute-start.14 = (f32[2,4096]{1,0:T(2,128)S(1)}, f32[2,4096]{1,0:T(2,128)S(1)}, u32[]{:S(2)}, u32[]{:S(2)}) collective-permute-start(f32[2,4096]{1,0:T(2,128)S(1)} %collective-permute-done.13), channel_id=1, source_target_pairs={{0,1},{1,2},{2,3},{3,4},{4,5},{5,6},{6,7},{7,8},{8,9},{9,10},{10,1... | collective-permute-start | bytes 98312 | tf_op jit(solution)/shard_map/ppermute | solution.py:42
  94.3 13.4 %copy-start.5 = (s32[2,8192]{1,0:T(2,128)S(1)}, s32[2,8192]{1,0:T(2,128)}, u32[]{:S(2)}) copy-start(s32[2,8192]{1,0:T(2,128)} %param.14) | copy-start | bytes 196612
  94.3 13.7 %copy-start.4 = (f32[2,4096]{1,0:T(2,128)S(1)}, f32[2,4096]{1,0:T(2,128)}, u32[]{:S(2)}) copy-start(f32[2,4096]{1,0:T(2,128)} %param.13) | copy-start | bytes 98308
  207.3 2.1 copy-start.2
  207.3 1.4 copy-start.3
  259.2 2.9 copy-start.7
  378.3 15.1 %copy-start.6 = (f32[2,64,64]{2,1,0:T(8,128)S(1)}, f32[2,64,64]{2,1,0:T(8,128)}, u32[]{:S(2)}) copy-start(f32[2,64,64]{2,1,0:T(8,128)} %param.25) | copy-start | bytes 98308
  378.3 334.3 %copy-start.9 = (s32[64]{0:T(128)S(1)}, s32[64]{0:T(128)}, u32[]{:S(2)}) copy-start(s32[64]{0:T(128)} %get-tuple-element.12) | copy-start | bytes 772
  394.1 321.5 %copy-start.1 = (bf16[64,32,128]{2,1,0:T(8,128)(2,1)S(1)}, bf16[64,32,128]{2,1,0:T(8,128)(2,1)}, u32[]{:S(2)}) copy-start(bf16[64,32,128]{2,1,0:T(8,128)(2,1)} %param.22) | copy-start | bytes 1572868
Sparse Core Ops, SparseCore 0:
  378.4 331.7 reduce-scatter.1
